TPU v7x, 128 devices: a whole 4x4x4 slice. The times are simulated.
128 devices in a mesh: src: 16 (over z_hi, x, core), snode: 8 (over y, z_lo).
Axes of the slice: x: 4, y: 4, z: 4 (z_hi: 2, z_lo: 2; z = z_hi * 2 + z_lo), core: 2. Of those that a mesh axis runs over, the one named last changes fastest.
Arguments:
- leaf_rhs: float32 [64, 256, 2048], P('snode', None, 'src'), may hold values from -6 to 6
- top_rhs: float32 [2048, 2048], P(None, 'src'), may hold values from -6 to 6
- leaf_inv: float32 [64, 256, 256], P('snode'), may hold values from -1 to 1, as said below
- coupling: float32 [64, 2048, 256], P('snode'), may hold values from -0.046875 to 0.046875
- top_inv: float32 [2048, 2048], P('snode'), may hold values from -1 to 1, as said below
- cond: float32 [64, 256], P('snode'), may hold values from 0.1 to 3
- electrodes: int32 [8192, 4], P('src'), may hold values from 0 to 2047, all different within a row
- blocks: int32 [16, 8192], P(None, 'src'), may hold values from 0 to 63
Outputs:
- sens: float32 [16, 256, 8192], P('snode', None, 'src')
Inputs may be any that keep to these rules, and one draw needn't show every extreme that they name: `electrodes`: the four sources of a row are different. `leaf_inv`: zero above the diagonal of each block. `top_inv`: zero above the diagonal.
All inputs are finite; a program needn't handle non-finite values.
Results may differ from a plain program's by a relative error of at most 0.00011.
Values sent between devices are 32-bit elements; how exact they have to be, the bound alone decides.
No kernel may reach another device: no remote copies, remote signals or barrier semaphores. Data moves between devices by JAX's collectives and lax.ppermute only.
A program may use at most 320 MiB of HBM per device.

v0:
```python
import jax
import jax.numpy as jnp
from jax import lax
from jax.sharding import PartitionSpec as P


def local(leaf_rhs, top_rhs, leaf_inv, coupling, top_inv, cond, electrodes, blocks):
    highest = lax.Precision.HIGHEST
    forward_leaf = jnp.einsum("bij,bjs->bis", leaf_inv, leaf_rhs, precision=highest)
    partial_value = jnp.einsum("bti,bis->ts", coupling, forward_leaf, precision=highest)
    coupled = lax.psum(partial_value, "snode")
    residual = top_rhs - coupled
    forward_top = jnp.dot(top_inv, residual, precision=highest)
    top_partial = jnp.einsum("rt,rs->ts", top_inv, forward_top, precision=highest)
    separator_field = lax.psum(top_partial, "snode")
    adjusted = forward_leaf - jnp.einsum(
        "bti,ts->bis", coupling, separator_field, precision=highest
    )
    leaf_field = jnp.einsum("bji,bjs->bis", leaf_inv, adjusted, precision=highest)
    leaves = leaf_field.shape[0]
    cells_n = leaf_field.shape[1]
    quads_n = electrodes.shape[0]
    shard_piece = lax.all_gather(leaf_field, "src", axis=2, tiled=True)
    width_n = shard_piece.shape[2]
    source_ids = lax.broadcasted_iota(jnp.int32, (width_n, quads_n), 0)

    def signed(plus_ids, minus_ids):
        upper = (source_ids == plus_ids[None, :]).astype(jnp.float32)
        lower = (source_ids == minus_ids[None, :]).astype(jnp.float32)
        return upper - lower

    current_sel = signed(electrodes[:, 0], electrodes[:, 1])
    potential_sel = signed(electrodes[:, 2], electrodes[:, 3])
    current_add = jnp.einsum("bcs,sq->bcq", shard_piece, current_sel, precision=highest)
    potential_add = jnp.einsum("bcs,sq->bcq", shard_piece, potential_sel, precision=highest)
    product = current_add * potential_add
    weighted = cond[:, :, None] * product
    owner_id = lax.axis_index("snode")
    local_blocks = blocks - owner_id * leaves
    own_rows = blocks.shape[0] // lax.axis_size("snode")
    summed = jnp.zeros((own_rows * lax.axis_size("snode"), cells_n, quads_n), jnp.float32)
    for leaf_id in range(leaves):
        summed = summed + jnp.where(
            (local_blocks == leaf_id)[:, None, :], weighted[leaf_id][None], 0.0
        )
    return lax.psum_scatter(summed, "snode", scatter_dimension=0, tiled=True)


def solution(mesh):
    return jax.shard_map(
        local,
        mesh=mesh,
        in_specs=(
            P("snode", None, "src"),
            P(None, "src"),
            P("snode", None, None),
            P("snode", None, None),
            P("snode", None),
            P("snode", None),
            P("src", None),
            P(None, "src"),
        ),
        out_specs=P("snode", None, "src"),
        check_vma=False,
    )
```

profile of v0, /device:TPU:1, one launch (start us, length us, event | category | flops | bytes accessed | tf_op | source)
XLA Modules:
  0.0 582.9 jit_solution(11139085248551137085)
XLA Ops:
  6.5 1.6 copy-done
  8.1 3.2 fusion.21
  11.3 17.3 %convolution_bitcast_fusion = f32[2048,128]{1,0:T(8,128)} fusion(f32[8,256,128]{2,1,0:T(8,128)S(1)} %fusion.21, f32[8,2048,256]{2,1,0:T(8,128)} %param.11), kind=kOutput, calls=%fused_computation.16 | convolution fusion | flops 6442450944 | bytes 18874368 | tf_op jit(solution)/shard_map/bti,bis->ts/dot_general | solution.py:10
  28.6 0.0 all-reduce.3.cloned.1.call-update
  28.6 0.0 all-reduce.5.cloned.1.call-start
  28.6 76.9 %all-reduce.3.cloned.1.call-done = f32[2048,128]{1,0:T(8,128)} async-done(((f32[2048,128]{1,0:T(8,128)}), f32[2048,128]{1,0:T(8,128)}) %all-reduce.3.cloned.1.call-update) | async-done | bytes 1048592 | tf_op jit(solution)/shard_map/psum | solution.py:11
  105.6 4.2 fusion.18
  109.8 2.2 convolution_bitcast_fusion.1
  112.0 0.0 all-reduce.5.cloned.1.call-update
  112.0 0.3 all-gather.2.cloned.1.call-start
  112.3 77.3 %all-reduce.5.cloned.1.call-done = f32[2048,128]{0,1:T(8,128)} async-done(((f32[2048,128]{0,1:T(8,128)}), f32[2048,128]{0,1:T(8,128)}) %all-reduce.5.cloned.1.call-update) | async-done | bytes 1048592 | tf_op jit(solution)/shard_map/psum | solution.py:15
  189.6 29.2 %fusion.16 = f32[8,256,128]{2,1,0:T(8,128)S(1)} fusion(f32[8,256,128]{2,1,0:T(8,128)S(1)} %fusion.21, f32[8,2048,256]{2,1,0:T(8,128)} %param.11, f32[2048,128]{0,1:T(8,128)} %all-reduce.5.cloned.1.call-done), kind=kOutput, calls=%fused_computation.24 | convolution fusion | flops 6442713088 | bytes 19922944 | tf_op jit(solution)/shard_map/bti,ts->bis/dot_general | solution.py:16
  218.8 0.0 copy-start.4
  218.9 0.0 copy-start.3
  218.9 3.0 convolution_bitcast_fusion.2
  221.9 0.0 all-gather.2.cloned.1.call-update
  221.9 0.6 reduce-scatter.2.cloned.1.call-start
  222.6 113.9 %all-gather.2.cloned.1.call-done = f32[8,256,2048]{1,2,0:T(8,128)} async-done(((f32[8,256,128]{1,2,0:T(8,128)}), f32[8,256,2048]{1,2,0:T(8,128)}) %all-gather.2.cloned.1.call-update) | async-done | bytes 16777232 | tf_op jit(solution)/shard_map/all_gather | solution.py:23
  336.5 32.1 %fusion = f32[8,256,512]{2,1,0:T(8,128)S(1)} fusion(f32[8,256,2048]{1,2,0:T(8,128)} %all-gather.2.cloned.1.call-done, s32[512]{0:T(512)S(1)} %bitcast.57, s32[512]{0:T(512)S(1)} %bitcast.58), kind=kOutput, calls=%fused_computation.1 | convolution fusion | flops 25775046656 | bytes 20975616 | tf_op jit(solution)/shard_map/bcs,sq->bcq/dot_general | solution.py:35
  368.6 30.3 %multiply_multiply_fusion = f32[8,256,512]{2,1,0:T(8,128)S(1)} fusion(f32[8,256,512]{2,1,0:T(8,128)S(1)} %fusion, f32[8,256,2048]{1,2,0:T(8,128)S(1)} %copy-done.5, s32[512]{0:T(512)S(1)} %bitcast.56, s32[512]{0:T(512)S(1)} %bitcast.55, f32[8,256]{1,0:T(8,128)S(1)} %copy-done.6), kind=kOutput, calls=%fused_computation.5 | convolution fusion | flops 25777143808 | bytes 25178112 | tf_op jit(solution)/shard_map/bcs,sq->bcq/dot_general | solution.py:34
  398.9 0.5 slice_bitcast_fusion.7
  399.3 10.2 %select_add_fusion = f32[16,256,512]{2,1,0:T(8,128)} fusion(f32[256,512]{1,0:T(8,128)S(1)} %get-tuple-element.6, f32[256,512]{1,0:T(8,128)S(1)} %get-tuple-element.7, f32[256,512]{1,0:T(8,128)S(1)} %get-tuple-element.8, f32[256,512]{1,0:T(8,128)S(1)} %get-tuple-element.9, f32[256,512]{1,0:T(8,128)S(1)} %get-tuple-element.10, ...), kind=kLoop, calls=%fused_computation | loop fusion | flops 31457280 | bytes 12648448 | tf_op jit(solution)/shard_map/add | solution.py:43
  409.5 0.0 reduce-scatter.2.cloned.1.call-update
  409.5 166.6 %reduce-scatter.2.cloned.1.call-done = f32[2,256,512]{2,1,0:T(8,128)} async-done(((f32[16,256,512]{2,1,0:T(8,128)}), f32[2,256,512]{2,1,0:T(8,128)}) %reduce-scatter.2.cloned.1.call-update) | async-done | bytes 1048592 | tf_op jit(solution)/shard_map/reduce_scatter | solution.py:46
  (14 shorter events, 0.1 us)
Async XLA Ops:
  6.5 1.6 copy-start
  6.5 99.0 %all-reduce.3.cloned.1.call-start = ((), (), s32[]{:S(2)}) async-start(), calls=%async_computation.1 | async-start | bytes 2097152 | tf_op jit(solution)/shard_map/psum | solution.py:11
  28.6 161.1 %all-reduce.5.cloned.1.call-start = ((), (), s32[]{:S(2)}) async-start(), calls=%async_computation.2 | async-start | bytes 2097152 | tf_op jit(solution)/shard_map/psum | solution.py:15
  105.5 4.2 copy-start.2
  112.0 224.5 %all-gather.2.cloned.1.call-start = ((), (), s32[]{:S(2)}) async-start(), calls=%async_computation.3 | async-start | bytes 17825792 | tf_op jit(solution)/shard_map/all_gather | solution.py:23
  218.8 3.6 copy-start.4
  218.9 3.6 copy-start.3
  221.9 354.2 %reduce-scatter.2.cloned.1.call-start = ((), (), s32[]{:S(2)}) async-start(), calls=%async_computation.4 | async-start | bytes 9437184 | tf_op jit(solution)/shard_map/reduce_scatter | solution.py:46
  336.5 32.1 %copy-start.5 = (f32[8,256,2048]{1,2,0:T(8,128)S(1)}, f32[8,256,2048]{1,2,0:T(8,128)}, u32[]{:S(2)}) copy-start(f32[8,256,2048]{1,2,0:T(8,128)} %all-gather.2.cloned.1.call-done) | copy-start | bytes 50331652
  336.5 32.1 %copy-start.6 = (f32[8,256]{1,0:T(8,128)S(1)}, f32[8,256]{1,0:T(8,128)}, u32[]{:S(2)}) copy-start(f32[8,256]{1,0:T(8,128)} %param.13) | copy-start | bytes 24580
  409.5 166.6 %copy-start.1 = (f32[8,256,256]{2,1,0:T(8,128)S(1)}, f32[8,256,256]{2,1,0:T(8,128)}, u32[]{:S(2)}) copy-start(f32[8,256,256]{2,1,0:T(8,128)} %param.10) | copy-start | bytes 6291460
Sparse Core Ops, SparseCore 0:
  28.7 76.7 all-reduce.2
  112.1 77.4 all-reduce.4
  222.0 114.4 all-gather.1
  409.7 166.3 reduce-scatter.1
where the time goes:
time: 590 us; the launch traced here: 583 us
  waiting for transfers between devices  435 us (74%)
  matrix products  121 us (21%)
  between operations  13.5 us (2%)
  other arithmetic  10.2 us (2%)
    reduce_scatter x1, waiting for transfers between devices, local(): return lax.psum_scatter(summed, 'snode', scatter_dimension=0, tiled=True)  167 us
    all_gather x1, waiting for transfers between devices, local(): shard_piece = lax.all_gather(leaf_field, 'src', axis=2, tiled=True)  114 us
    psum x1, waiting for transfers between devices, local(): separator_field = lax.psum(top_partial, 'snode')  77.3 us
    psum x1, waiting for transfers between devices, local(): coupled = lax.psum(partial_value, 'snode')  76.9 us
    dot_general x1, matrix products, local(): jnp.einsum('bcs,sq->bcq', shard_piece, potential_sel, precision=highest)  32.1 us
    dot_general x1, matrix products, local(): jnp.einsum('bcs,sq->bcq', shard_piece, current_sel, precision=highest)  30.3 us
    dot_general x1, matrix products, local(): jnp.einsum('bti,ts->bis', coupling, separator_field, precision=highest)  29.2 us
    dot_general x1, matrix products, local(): jnp.einsum('bti,bis->ts', coupling, forward_leaf, precision=highest)  17.3 us
  transfers between devices with their start and end apart: 4, of which 4 were waited for; matrix products, arithmetic and copies ran while one was open for 0% of the time, Pallas kernels for 0%

commit v1 on v0

--- a/solution.py
+++ b/solution.py
@@ -4,11 +4,16 @@
 from jax.sharding import PartitionSpec as P
 
 
+def gather_and_add(array, name):
+    terms = lax.all_gather(array, name)
+    return jnp.sum(terms, axis=0)
+
+
 def local(leaf_rhs, top_rhs, leaf_inv, coupling, top_inv, cond, electrodes, blocks):
     highest = lax.Precision.HIGHEST
     forward_leaf = jnp.einsum("bij,bjs->bis", leaf_inv, leaf_rhs, precision=highest)
     partial_value = jnp.einsum("bti,bis->ts", coupling, forward_leaf, precision=highest)
-    coupled = lax.psum(partial_value, "snode")
+    coupled = gather_and_add(partial_value, "snode")
     residual = top_rhs - coupled
     forward_top = jnp.dot(top_inv, residual, precision=highest)
     top_partial = jnp.einsum("rt,rs->ts", top_inv, forward_top, precision=highest)

time: 590 us -> 698 us (1.18)
  waiting for transfers between devices: 435 us -> 529 us
  local copies, waits for them, and re-layouts: 2.08 us -> 14.5 us
    all_gather x0 -> x1, waiting for transfers between devices: none -> 169 us  [gather_and_add(): terms = lax.all_gather(array, name)]
    psum x1 -> x0, waiting for transfers between devices: 76.9 us -> none  [local(): coupled = lax.psum(partial_value, 'snode')]
    unnamed x14 -> x18, local copies, waits for them, and re-layouts: 1.62 us -> 14 us
where the time goes in v1:
time: 698 us; the launch traced here: 694 us
  waiting for transfers between devices  529 us (76%)
  matrix products  124 us (18%)
  local copies, waits for them, and re-layouts  14.5 us (2%)
  between operations  13.6 us (2%)
  other arithmetic  12.3 us (2%)
    all_gather x1, waiting for transfers between devices, gather_and_add(): terms = lax.all_gather(array, name)  169 us
    reduce_scatter x1, waiting for transfers between devices, local(): return lax.psum_scatter(summed, 'snode', scatter_dimension=0, tiled=True)  167 us
    all_gather x1, waiting for transfers between devices, local(): shard_piece = lax.all_gather(leaf_field, 'src', axis=2, tiled=True)  114 us
    psum x1, waiting for transfers between devices, local(): separator_field = lax.psum(top_partial, 'snode')  79.2 us
    dot_general x1, matrix products, local(): jnp.einsum('bcs,sq->bcq', shard_piece, potential_sel, precision=highest)  32.1 us
    dot_general x1, matrix products, local(): jnp.einsum('bcs,sq->bcq', shard_piece, current_sel, precision=highest)  30.4 us
    dot_general x1, matrix products, local(): jnp.einsum('bti,ts->bis', coupling, separator_field, precision=highest)  29.2 us
    dot_general x1, matrix products, local(): jnp.einsum('bti,bis->ts', coupling, forward_leaf, precision=highest)  21.2 us
  transfers between devices with their start and end apart: 4, of which 4 were waited for; matrix products, arithmetic and copies ran while one was open for 0% of the time, Pallas kernels for 0%

profile of v1, /device:TPU:1, one launch (start us, length us, event | category | flops | bytes accessed | tf_op | source)
XLA Modules:
  0.0 693.6 jit_solution(3814288037586335014)
XLA Ops:
  6.5 1.6 copy-done
  8.1 3.2 fusion.21
  11.3 21.2 %convolution_bitcast_fusion = f32[2048,128]{0,1:T(8,128)} fusion(f32[8,256,128]{2,1,0:T(8,128)S(1)} %fusion.21, f32[8,2048,256]{2,1,0:T(8,128)} %param.11), kind=kOutput, calls=%fused_computation.17 | convolution fusion | flops 6442450944 | bytes 18874368 | tf_op jit(solution)/shard_map/bti,bis->ts/dot_general | solution.py:15
  32.5 0.0 all-gather.6.cloned.1.call-update
  32.6 0.6 all-reduce.2.cloned.1.call-start
  33.1 2.5 copy.14
  35.7 168.7 %all-gather.6.cloned.1.call-done = f32[16384,128]{0,1:T(8,128)} async-done(((f32[2048,128]{0,1:T(8,128)}), f32[16384,128]{0,1:T(8,128)}) %all-gather.6.cloned.1.call-update) | async-done | bytes 8388624 | tf_op jit(solution)/shard_map/all_gather | solution.py:8
  204.3 9.9 %copy.22 = f32[16,8,8,2048]{3,2,1,0:T(8,128)S(1)} copy(f32[16,8,8,2048]{3,1,2,0:T(8,128)} %bitcast.60) | data formatting | bytes 16777216
  214.2 2.0 bitcast_reduce_fusion
  216.2 2.2 fusion.18
  218.5 2.4 convolution_bitcast_fusion.1
  220.9 0.0 all-reduce.2.cloned.1.call-update
  220.9 0.0 all-gather.4.cloned.1.call-start
  220.9 79.2 %all-reduce.2.cloned.1.call-done = f32[2048,128]{0,1:T(8,128)} async-done(((f32[2048,128]{0,1:T(8,128)}), f32[2048,128]{0,1:T(8,128)}) %all-reduce.2.cloned.1.call-update) | async-done | bytes 1048592 | tf_op jit(solution)/shard_map/psum | solution.py:20
  300.1 29.2 %fusion.16 = f32[8,256,128]{2,1,0:T(8,128)S(1)} fusion(f32[8,256,128]{2,1,0:T(8,128)S(1)} %fusion.21, f32[8,2048,256]{2,1,0:T(8,128)} %param.11, f32[2048,128]{0,1:T(8,128)} %all-reduce.2.cloned.1.call-done), kind=kOutput, calls=%fused_computation.25 | convolution fusion | flops 6442713088 | bytes 19922944 | tf_op jit(solution)/shard_map/bti,ts->bis/dot_general | solution.py:21
  329.3 3.0 convolution_bitcast_fusion.2
  332.3 0.3 reduce-scatter.2.cloned.1.call-start
  332.7 114.2 %all-gather.4.cloned.1.call-done = f32[8,256,2048]{1,2,0:T(8,128)} async-done(((f32[8,256,128]{1,2,0:T(8,128)}), f32[8,256,2048]{1,2,0:T(8,128)}) %all-gather.4.cloned.1.call-update) | async-done | bytes 16777232 | tf_op jit(solution)/shard_map/all_gather | solution.py:28
  446.9 32.1 %fusion = f32[8,256,512]{2,1,0:T(8,128)S(1)} fusion(f32[8,256,2048]{1,2,0:T(8,128)} %all-gather.4.cloned.1.call-done, s32[512]{0:T(512)S(1)} %bitcast.63, s32[512]{0:T(512)S(1)} %bitcast.64), kind=kOutput, calls=%fused_computation.2 | convolution fusion | flops 25775046656 | bytes 20975616 | tf_op jit(solution)/shard_map/bcs,sq->bcq/dot_general | solution.py:40
  479.0 30.4 %multiply_multiply_fusion = f32[8,256,512]{2,1,0:T(8,128)S(1)} fusion(f32[8,256,512]{2,1,0:T(8,128)S(1)} %fusion, f32[8,256,2048]{1,2,0:T(8,128)S(1)} %copy-done.6, s32[512]{0:T(512)S(1)} %bitcast.62, s32[512]{0:T(512)S(1)} %bitcast.61, f32[8,256]{1,0:T(8,128)S(1)} %copy-done.7), kind=kOutput, calls=%fused_computation.6 | convolution fusion | flops 25777143808 | bytes 25178112 | tf_op jit(solution)/shard_map/bcs,sq->bcq/dot_general | solution.py:39
  509.4 0.5 slice_bitcast_fusion.7
  509.9 10.3 %select_add_fusion = f32[16,256,512]{2,1,0:T(8,128)} fusion(f32[256,512]{1,0:T(8,128)S(1)} %get-tuple-element.6, f32[256,512]{1,0:T(8,128)S(1)} %get-tuple-element.7, f32[256,512]{1,0:T(8,128)S(1)} %get-tuple-element.8, f32[256,512]{1,0:T(8,128)S(1)} %get-tuple-element.9, f32[256,512]{1,0:T(8,128)S(1)} %get-tuple-element.10, ...), kind=kLoop, calls=%fused_computation.1 | loop fusion | flops 31457280 | bytes 12648448 | tf_op jit(solution)/shard_map/add | solution.py:48
  520.1 0.0 reduce-scatter.2.cloned.1.call-update
  520.1 166.6 %reduce-scatter.2.cloned.1.call-done = f32[2,256,512]{2,1,0:T(8,128)} async-done(((f32[16,256,512]{2,1,0:T(8,128)}), f32[2,256,512]{2,1,0:T(8,128)}) %reduce-scatter.2.cloned.1.call-update) | async-done | bytes 1048592 | tf_op jit(solution)/shard_map/reduce_scatter | solution.py:51
  (19 shorter events, 0.1 us)
Async XLA Ops:
  6.5 1.6 copy-start
  6.5 197.8 %all-gather.6.cloned.1.call-start = ((), (), s32[]{:S(2)}) async-start(), calls=%async_computation.4 | async-start | bytes 9437184 | tf_op jit(solution)/shard_map/all_gather | solution.py:8
  32.6 267.5 %all-reduce.2.cloned.1.call-start = ((), (), s32[]{:S(2)}) async-start(), calls=%async_computation.1 | async-start | bytes 2097152 | tf_op jit(solution)/shard_map/psum | solution.py:20
  214.2 2.0 copy-start.2
  214.2 2.0 copy-start.3
  220.9 226.0 %all-gather.4.cloned.1.call-start = ((), (), s32[]{:S(2)}) async-start(), calls=%async_computation.2 | async-start | bytes 17825792 | tf_op jit(solution)/shard_map/all_gather | solution.py:28
  329.3 3.3 copy-start.5
  329.3 3.3 copy-start.4
  332.3 354.4 %reduce-scatter.2.cloned.1.call-start = ((), (), s32[]{:S(2)}) async-start(), calls=%async_computation.3 | async-start | bytes 9437184 | tf_op jit(solution)/shard_map/reduce_scatter | solution.py:51
  446.9 32.1 %copy-start.6 = (f32[8,256,2048]{1,2,0:T(8,128)S(1)}, f32[8,256,2048]{1,2,0:T(8,128)}, u32[]{:S(2)}) copy-start(f32[8,256,2048]{1,2,0:T(8,128)} %all-gather.4.cloned.1.call-done) | copy-start | bytes 50331652
  446.9 32.1 %copy-start.7 = (f32[8,256]{1,0:T(8,128)S(1)}, f32[8,256]{1,0:T(8,128)}, u32[]{:S(2)}) copy-start(f32[8,256]{1,0:T(8,128)} %param.13) | copy-start | bytes 24580
  520.1 166.6 %copy-start.1 = (f32[8,256,256]{2,1,0:T(8,128)S(1)}, f32[8,256,256]{2,1,0:T(8,128)}, u32[]{:S(2)}) copy-start(f32[8,256,256]{2,1,0:T(8,128)} %param.10) | copy-start | bytes 6291460
Sparse Core Ops, SparseCore 0:
  32.7 171.5 all-gather.5
  221.0 79.0 all-reduce.1
  332.5 114.4 all-gather.3
  520.3 166.3 reduce-scatter.1
